TPU v7x, 32 devices: a whole 2x2x4 slice. The times are simulated.
32 devices in a mesh: dp: 4 (over y, x), fsdp: 8 (over z, core).
Axes of the slice: x: 2, y: 2, z: 4, core: 2. Of those that a mesh axis runs over, the one named last changes fastest.
Arguments:
- inputs: bfloat16 [2, 16384, 512], P(None, ('dp', 'fsdp')), may hold values from -6 to 6
- memory: bfloat16 [2, 16384, 512], P(None, ('dp', 'fsdp')), may hold values from -6 to 6
- cotangent: bfloat16 [2, 16384, 512], P(None, ('dp', 'fsdp')), may hold values from -6 to 6
- lengths: int32 [2, 32, 2, 32], P(None, ('dp', 'fsdp')), may hold values from 0 to 512, as said below
- stacked_weights: float32 [8, 512, 512], P(None, 'fsdp')
- expand_weights: float32 [512, 2048], P('fsdp'), may hold values from -0.25 to 0.25
- contract_weights: float32 [2048, 512], P('fsdp'), may hold values from -0.125 to 0.125
- scale_vectors: float32 [9, 512], P(None, 'fsdp'), as said below
- stacked_first: float32 [8, 512, 512], P(None, 'fsdp'), may hold values from -434.4464 to 434.4464
- stacked_second: float32 [8, 512, 512], P(None, 'fsdp'), may hold values from 655.36 to 32768
- expand_first: float32 [512, 2048], P('fsdp'), may hold values from -434.4464 to 434.4464
- expand_second: float32 [512, 2048], P('fsdp'), may hold values from 655.36 to 32768
- contract_first: float32 [2048, 512], P('fsdp'), may hold values from -434.4464 to 434.4464
- contract_second: float32 [2048, 512], P('fsdp'), may hold values from 655.36 to 32768
- vector_first: float32 [9, 512], P(None, 'fsdp'), may hold values from -434.4464 to 434.4464
- vector_second: float32 [9, 512], P(None, 'fsdp'), may hold values from 655.36 to 32768
Outputs:
- output: bfloat16 [2, 16384, 512], P(None, ('dp', 'fsdp'))
- input_grad: float32 [2, 16384, 512], P(None, ('dp', 'fsdp'))
- memory_grad: float32 [2, 16384, 512], P(None, ('dp', 'fsdp'))
- stacked_next: float32 [8, 512, 512], P(None, 'fsdp')
- expand_next: float32 [512, 2048], P('fsdp')
- contract_next: float32 [2048, 512], P('fsdp')
- vector_next: float32 [9, 512], P(None, 'fsdp')
- stacked_first_next: float32 [8, 512, 512], P(None, 'fsdp')
- stacked_second_next: float32 [8, 512, 512], P(None, 'fsdp')
- expand_first_next: float32 [512, 2048], P('fsdp')
- expand_second_next: float32 [512, 2048], P('fsdp')
- contract_first_next: float32 [2048, 512], P('fsdp')
- contract_second_next: float32 [2048, 512], P('fsdp')
- vector_first_next: float32 [9, 512], P(None, 'fsdp')
- vector_second_next: float32 [9, 512], P(None, 'fsdp')
Inputs may be any that keep to these rules, and one draw needn't show every extreme that they name: In every micro-batch exactly half of the slabs, drawn from the seed, hold one document pair: entry 0 of both sides is 512, the others 0. In the other slabs the target entries are sentence lengths of 16 to 63, except the last nonzero one, which may be shorter, and the memory side holds the same nonzero lengths in reverse order. Each side of each slab sums to 512. `scale_vectors`: rows 6 to 8 are positive.
All inputs are finite; a program needn't handle non-finite values.
Results may differ from a plain program's by a relative error of at most 0.02.
Values may be sent and summed in bfloat16 or wider, within the bound.
No kernel may reach another device: no remote copies, remote signals or barrier semaphores. Data moves between devices by JAX's collectives and lax.ppermute only.
A program may use at most 192 MiB of HBM per device.

v0:
```python
import jax
import jax.numpy as jnp
from jax import lax
from jax.sharding import PartitionSpec as P

HEADS = 8
HEAD = 64
SLAB = 512
STEP = 3


NORM_EPS = 1e-05
ADAM_EPS = 1e-08
LEARN_RATE = 0.2
FAR_BELOW = -1e30


def shortened(array):
    return jax.tree.map(lambda a: a.astype(jnp.bfloat16) if a.dtype == jnp.float32 else a, array)


def product(left_side, right_side):
    return jnp.dot(left_side, right_side, preferred_element_type=jnp.float32)


def across(left_side, right_side):
    return lax.dot_general(
        left_side, right_side, (((0,), (0,)), ((), ())), preferred_element_type=jnp.float32
    )


def against(left_side, right_side):
    return lax.dot_general(
        left_side, right_side, (((1,), (1,)), ((), ())), preferred_element_type=jnp.float32
    )


def normalize(residual, gain_row, shift_row):
    centred = residual - jnp.mean(residual, axis=-1, keepdims=True)
    spread = jnp.mean(centred * centred, axis=-1, keepdims=True)
    return centred * lax.rsqrt(spread + NORM_EPS) * gain_row + shift_row


def settle(residual, branch, omega_row, gain_row, shift_row):
    return normalize(omega_row * residual + branch, gain_row, shift_row)


def smooth(values):
    return jax.nn.gelu(values, approximate=True)


def segments(piece_lengths, row_count):
    closing = jnp.cumsum(piece_lengths, axis=-1)
    places = jnp.arange(row_count, dtype=jnp.int32)
    return jnp.sum(
        (closing[:, None, :] <= places[None, :, None]).astype(jnp.int32), axis=-1, dtype=jnp.int32
    )


def make_masks(piece_lengths, row_count):
    labels = segments(piece_lengths, row_count)
    places = jnp.arange(row_count, dtype=jnp.int32)
    self_allowed = (labels[0][:, None] == labels[0][None, :]) & (places[None, :] <= places[:, None])
    cross_allowed = labels[0][:, None] == labels[1][None, :]
    return (self_allowed, cross_allowed)


def split_heads(rows):
    return rows.reshape(rows.shape[0], HEADS, HEAD)


def masked_scores(queries, key_rows, allowed):
    scores = jnp.einsum(
        "qhd,khd->hqk",
        split_heads(queries),
        split_heads(key_rows),
        preferred_element_type=jnp.float32,
    ) * HEAD ** (-0.5)
    return jnp.where(allowed[None], scores, FAR_BELOW)


def attend(queries, key_rows, value_rows, allowed):
    scores = masked_scores(queries, key_rows, allowed)
    row_top = jnp.max(scores, axis=-1, keepdims=True)
    exponent = jnp.exp(scores - row_top)
    row_total = jnp.sum(exponent, axis=-1, keepdims=True)
    probabilities = (exponent / row_total).astype(jnp.bfloat16)
    mixture = jnp.einsum(
        "hqk,khd->qhd", probabilities, split_heads(value_rows), preferred_element_type=jnp.float32
    )
    return (mixture.reshape(queries.shape[0], HEADS * HEAD), row_top + jnp.log(row_total))


def attend_back(queries, key_rows, value_rows, allowed, log_total, upstream):
    probabilities = jnp.exp(masked_scores(queries, key_rows, allowed) - log_total)
    upstream_heads = split_heads(upstream)
    prob_grad = jnp.einsum(
        "qhd,khd->hqk", upstream_heads, split_heads(value_rows), preferred_element_type=jnp.float32
    )
    value_grad = jnp.einsum(
        "hqk,qhd->khd",
        probabilities.astype(jnp.bfloat16),
        upstream_heads,
        preferred_element_type=jnp.float32,
    )
    centre = jnp.sum(prob_grad * probabilities, axis=-1, keepdims=True)
    score_grad = (probabilities * (prob_grad - centre)).astype(jnp.bfloat16)
    query_grad = jnp.einsum(
        "hqk,khd->qhd", score_grad, split_heads(key_rows), preferred_element_type=jnp.float32
    ) * HEAD ** (-0.5)
    key_grad = jnp.einsum(
        "hqk,qhd->khd", score_grad, split_heads(queries), preferred_element_type=jnp.float32
    ) * HEAD ** (-0.5)
    query_count = queries.shape[0]
    key_count = key_rows.shape[0]
    return (
        query_grad.reshape(query_count, HEADS * HEAD).astype(jnp.bfloat16),
        key_grad.reshape(key_count, HEADS * HEAD).astype(jnp.bfloat16),
        value_grad.reshape(key_count, HEADS * HEAD).astype(jnp.bfloat16),
    )


def layer_forward(weights, tokens, memory_rows, piece_lengths):
    stacked, expand, contract, vector_rows = weights
    gain_rows = vector_rows.astype(jnp.float32)
    self_allowed, cross_allowed = make_masks(piece_lengths, tokens.shape[0])
    projected = jnp.einsum(
        "sd,jde->jse", tokens, stacked[0:3], preferred_element_type=jnp.float32
    ).astype(jnp.bfloat16)
    first_mix, first_log = attend(projected[0], projected[1], projected[2], self_allowed)
    first_mix = first_mix.astype(jnp.bfloat16)
    first_branch = product(first_mix, stacked[3])
    first_state = settle(
        tokens.astype(jnp.float32), first_branch, gain_rows[6], gain_rows[0], gain_rows[3]
    )
    first_low = first_state.astype(jnp.bfloat16)
    cross_queries = product(first_low, stacked[4]).astype(jnp.bfloat16)
    cross_pairs = jnp.einsum(
        "sd,jde->jse", memory_rows, stacked[5:7], preferred_element_type=jnp.float32
    ).astype(jnp.bfloat16)
    second_mix, second_log = attend(cross_queries, cross_pairs[0], cross_pairs[1], cross_allowed)
    second_mix = second_mix.astype(jnp.bfloat16)
    second_branch = product(second_mix, stacked[7])
    second_state = settle(first_state, second_branch, gain_rows[7], gain_rows[1], gain_rows[4])
    second_low = second_state.astype(jnp.bfloat16)
    hidden = product(second_low, expand)
    activated = smooth(hidden).astype(jnp.bfloat16)
    ffn_branch = product(activated, contract)
    output_now = settle(second_state, ffn_branch, gain_rows[8], gain_rows[2], gain_rows[5])
    kept = (
        projected,
        first_mix,
        first_log,
        first_branch,
        first_state,
        first_low,
        cross_queries,
        cross_pairs,
        second_mix,
        second_log,
        second_branch,
        second_state,
        second_low,
        hidden,
        activated,
        ffn_branch,
        self_allowed,
        cross_allowed,
        gain_rows,
    )
    return (output_now, kept)


def layer_backward(weights, tokens, memory_rows, piece_lengths, upstream):
    stacked, expand, contract, vector_rows = weights
    output_now, kept = layer_forward(weights, tokens, memory_rows, piece_lengths)
    (
        projected,
        first_mix,
        first_log,
        first_branch,
        first_state,
        first_low,
        cross_queries,
        cross_pairs,
        second_mix,
        second_log,
        second_branch,
        second_state,
        second_low,
        hidden,
        activated,
        ffn_branch,
        self_allowed,
        cross_allowed,
        gain_rows,
    ) = kept
    unused, settle_three = jax.vjp(
        settle, second_state, ffn_branch, gain_rows[8], gain_rows[2], gain_rows[5]
    )
    second_grad, ffn_grad, omega_three, gain_three, shift_three = settle_three(
        upstream.astype(jnp.float32)
    )
    ffn_low = ffn_grad.astype(jnp.bfloat16)
    contract_grad = across(activated, ffn_low)
    unused, smooth_back = jax.vjp(smooth, hidden)
    (hidden_grad,) = smooth_back(against(ffn_low, contract))
    hidden_low = hidden_grad.astype(jnp.bfloat16)
    expand_grad = across(second_low, hidden_low)
    second_grad = second_grad + against(hidden_low, expand)
    unused, settle_two = jax.vjp(
        settle, first_state, second_branch, gain_rows[7], gain_rows[1], gain_rows[4]
    )
    first_grad, branch_two, omega_two, gain_two, shift_two = settle_two(second_grad)
    branch_two = branch_two.astype(jnp.bfloat16)
    out_two_grad = across(second_mix, branch_two)
    mix_two = against(branch_two, stacked[7]).astype(jnp.bfloat16)
    cross_query_grad, cross_key_grad, cross_value_grad = attend_back(
        cross_queries, cross_pairs[0], cross_pairs[1], cross_allowed, second_log, mix_two
    )
    memory_grad = against(cross_key_grad, stacked[5]) + against(cross_value_grad, stacked[6])
    first_grad = first_grad + against(cross_query_grad, stacked[4])
    unused, settle_one = jax.vjp(
        settle, tokens.astype(jnp.float32), first_branch, gain_rows[6], gain_rows[0], gain_rows[3]
    )
    input_grad, branch_one, omega_one, gain_one, shift_one = settle_one(first_grad)
    branch_one = branch_one.astype(jnp.bfloat16)
    out_one_grad = across(first_mix, branch_one)
    mix_one = against(branch_one, stacked[3]).astype(jnp.bfloat16)
    self_grads = jnp.stack(
        attend_back(projected[0], projected[1], projected[2], self_allowed, first_log, mix_one)
    )
    projection_grads = jnp.einsum(
        "sd,jse->jde", tokens, self_grads, preferred_element_type=jnp.float32
    )
    input_grad = input_grad + jnp.einsum(
        "jse,jde->sd", self_grads, stacked[0:3], preferred_element_type=jnp.float32
    )
    stacked_grad = jnp.concatenate(
        [
            projection_grads,
            out_one_grad[None],
            across(first_low, cross_query_grad)[None],
            across(memory_rows, cross_key_grad)[None],
            across(memory_rows, cross_value_grad)[None],
            out_two_grad[None],
        ],
        axis=0,
    )
    vector_grad = jnp.stack(
        [
            gain_one,
            gain_two,
            gain_three,
            shift_one,
            shift_two,
            shift_three,
            omega_one,
            omega_two,
            omega_three,
        ]
    )
    return (input_grad, memory_grad, (stacked_grad, expand_grad, contract_grad, vector_grad))


def adam_update(weight, first_moment, second_moment, gradient, correction):
    first_next = 0.5 * first_moment + 0.5 * gradient
    second_next = 0.5 * second_moment + 0.5 * gradient * gradient
    weight_next = weight - LEARN_RATE * (first_next / correction) / (
        jnp.sqrt(second_next / correction) + ADAM_EPS
    )
    return (weight_next, first_next, second_next)


def per_device(
    inputs,
    memory,
    cotangent,
    lengths,
    stacked_weights,
    expand_weights,
    contract_weights,
    scale_vectors,
    stacked_first,
    stacked_second,
    expand_first,
    expand_second,
    contract_first,
    contract_second,
    vector_first,
    vector_second,
):
    shards = (
        stacked_weights.astype(jnp.bfloat16),
        expand_weights.astype(jnp.bfloat16),
        contract_weights.astype(jnp.bfloat16),
        scale_vectors.astype(jnp.bfloat16),
    )
    slab_count = lengths.shape[1]
    width = inputs.shape[2]

    def fetch_weights():
        return (
            lax.all_gather(shards[0], "fsdp", axis=1, tiled=True),
            lax.all_gather(shards[1], "fsdp", axis=0, tiled=True),
            lax.all_gather(shards[2], "fsdp", axis=0, tiled=True),
            lax.all_gather(shards[3], "fsdp", axis=1, tiled=True),
        )

    outputs = []
    input_grads = []
    memory_grads = []
    totals = None
    for micro_index in range(inputs.shape[0]):
        token_slabs = inputs[micro_index].reshape(slab_count, SLAB, width)
        memory_slabs = memory[micro_index].reshape(slab_count, SLAB, width)
        upstream_slabs = cotangent[micro_index].reshape(slab_count, SLAB, width)
        weights = fetch_weights()
        slab_index = 0
        output_now, unused = layer_forward(
            weights,
            token_slabs[slab_index],
            memory_slabs[slab_index],
            lengths[micro_index, slab_index],
        )
        slab_outputs = output_now.astype(jnp.bfloat16)
        outputs.append(slab_outputs)
        weights = fetch_weights()
        micro_grads = None
        slab_index = 0
        input_grad, memory_grad, local_grads = layer_backward(
            weights,
            token_slabs[slab_index],
            memory_slabs[slab_index],
            lengths[micro_index, slab_index],
            upstream_slabs[slab_index],
        )
        micro_grads = local_grads
        input_grads.append(input_grad)
        memory_grads.append(memory_grad)
        shard_grads = (
            lax.psum_scatter(micro_grads[0], "fsdp", scatter_dimension=1, tiled=True),
            lax.psum_scatter(micro_grads[1], "fsdp", scatter_dimension=0, tiled=True),
            lax.psum_scatter(micro_grads[2], "fsdp", scatter_dimension=0, tiled=True),
            lax.psum_scatter(micro_grads[3], "fsdp", scatter_dimension=1, tiled=True),
        )
        shard_grads = jax.tree.map(
            lambda part: part.astype(jnp.float32), lax.psum(shortened(shard_grads), "dp")
        )
        totals = shard_grads if totals is None else jax.tree.map(jnp.add, totals, shard_grads)
    correction = 1.0 - 0.5**STEP
    params = (stacked_weights, expand_weights, contract_weights, scale_vectors)
    firsts = (stacked_first, expand_first, contract_first, vector_first)
    seconds = (stacked_second, expand_second, contract_second, vector_second)
    updates = [
        adam_update(
            params[position], firsts[position], seconds[position], totals[position], correction
        )
        for position in range(4)
    ]
    return (
        jnp.stack(outputs),
        jnp.stack(input_grads),
        jnp.stack(memory_grads),
        updates[0][0],
        updates[1][0],
        updates[2][0],
        updates[3][0],
        updates[0][1],
        updates[0][2],
        updates[1][1],
        updates[1][2],
        updates[2][1],
        updates[2][2],
        updates[3][1],
        updates[3][2],
    )


def solution(mesh):
    return jax.shard_map(
        per_device,
        mesh=mesh,
        in_specs=(
            P(None, ("dp", "fsdp"), None),
            P(None, ("dp", "fsdp"), None),
            P(None, ("dp", "fsdp"), None),
            P(None, ("dp", "fsdp"), None, None),
            P(None, "fsdp", None),
            P("fsdp", None),
            P("fsdp", None),
            P(None, "fsdp"),
            P(None, "fsdp", None),
            P(None, "fsdp", None),
            P("fsdp", None),
            P("fsdp", None),
            P("fsdp", None),
            P("fsdp", None),
            P(None, "fsdp"),
            P(None, "fsdp"),
        ),
        out_specs=(
            P(None, ("dp", "fsdp"), None),
            P(None, ("dp", "fsdp"), None),
            P(None, ("dp", "fsdp"), None),
            P(None, "fsdp", None),
            P("fsdp", None),
            P("fsdp", None),
            P(None, "fsdp"),
            P(None, "fsdp", None),
            P(None, "fsdp", None),
            P("fsdp", None),
            P("fsdp", None),
            P("fsdp", None),
            P("fsdp", None),
            P(None, "fsdp"),
            P(None, "fsdp"),
        ),
        check_vma=False,
    )
```

profile of v0, /device:TPU:0, one launch (start us, length us, event | category | flops | bytes accessed | tf_op | source)
XLA Modules:
  0.0 678.3 jit_solution(16361738093834263019)
XLA Ops:
  14.3 15.8 %all-gather = bf16[8,64,9]{1,2,0:T(8,128)(2,1)S(1)} all-gather(bf16[1,64,9]{1,2,0:T(8,128)(2,1)S(1)} %convert_bitcast_fusion.2), channel_id=1, replica_groups=mesh['dp'=4,'fsdp'=8] {'fsdp'}, dimensions={0}, use_global_device_ids=true | all-gather | bytes 10368 | tf_op jit(solution)/shard_map/all_gather | solution.py:307
  32.4 27.8 %all-gather.5.cloned.1.call-done = bf16[8,512,512]{2,0,1:T(8,128)(2,1)} async-done(((bf16[8,64,512]{2,0,1:T(8,128)(2,1)}), bf16[8,512,512]{2,0,1:T(8,128)(2,1)}) %all-gather.5.cloned.1.call-update) | async-done | bytes 4194320 | tf_op jit(solution)/shard_map/all_gather | solution.py:304
  79.1 5.8 fusion.166
  113.0 5.2 fusion.146
  145.5 6.0 fusion.142
  151.6 5.8 fusion.21
  187.0 5.5 multiply_reduce_fusion.3
  208.0 5.7 multiply_reduce_fusion
  213.8 4.8 multiply_convert_fusion
  224.2 4.6 fusion.83
  230.9 4.4 bitcast_dynamic-update-slice_fusion
  248.9 10.5 %copy.319 = f32[8,512,512]{2,0,1:T(8,128)} copy(f32[8,512,512]{1,2,0:T(8,128)} %fusion.42) | data formatting | bytes 16777216 | tf_op jit(solution)/shard_map/concatenate | solution.py:239
  261.0 4.9 fusion.69
  266.9 5.5 multiply_reduce_fusion.2
  272.4 5.0 multiply_convert_fusion.2
  281.2 4.5 fusion.80
  304.8 10.5 %copy.314 = f32[8,512,512]{2,0,1:T(8,128)} copy(f32[8,512,512]{1,2,0:T(8,128)} %fusion.46) | data formatting | bytes 16777216 | tf_op jit(solution)/shard_map/concatenate | solution.py:239
  328.6 17.3 %reduce-scatter.17.cloned.1.call-done = f32[64,2048]{1,0:T(8,128)} async-done(((f32[512,2048]{1,0:T(8,128)}), f32[64,2048]{1,0:T(8,128)}) %reduce-scatter.17.cloned.1.call-update) | async-done | bytes 524304 | tf_op jit(solution)/shard_map/reduce_scatter | solution.py:343
  347.6 88.3 %reduce-scatter.15.cloned.1.call-done = f32[8,64,512]{2,0,1:T(8,128)} async-done(((f32[8,512,512]{2,0,1:T(8,128)}), f32[8,64,512]{2,0,1:T(8,128)}) %reduce-scatter.15.cloned.1.call-update) | async-done | bytes 1048592 | tf_op jit(solution)/shard_map/reduce_scatter | solution.py:342
  438.0 88.2 %reduce-scatter.13.cloned.1.call-done = f32[8,64,512]{2,0,1:T(8,128)} async-done(((f32[8,512,512]{2,0,1:T(8,128)}), f32[8,64,512]{2,0,1:T(8,128)}) %reduce-scatter.13.cloned.1.call-update) | async-done | bytes 1048592 | tf_op jit(solution)/shard_map/reduce_scatter | solution.py:342
  539.3 17.8 %reduce-scatter.25.cloned.1.call-done = f32[64,9]{1,0:T(8,128)} async-done(((f32[512,9]{1,0:T(8,128)}), f32[64,9]{1,0:T(8,128)}) %reduce-scatter.25.cloned.1.call-update) | async-done | bytes 2320
  557.9 30.0 %reduce-scatter.27.cloned.1.call-done = f32[64,9]{1,0:T(8,128)} async-done(((f32[512,9]{1,0:T(8,128)}), f32[64,9]{1,0:T(8,128)}) %reduce-scatter.27.cloned.1.call-update) | async-done | bytes 2320
  588.7 10.1 %all-reduce = (bf16[9,64]{1,0:T(8,128)(2,1)S(1)}, bf16[9,64]{1,0:T(8,128)(2,1)S(1)}) all-reduce(bf16[9,64]{1,0:T(8,128)(2,1)S(1)} %copy.358, bf16[9,64]{1,0:T(8,128)(2,1)S(1)} %copy.356), channel_id=1, replica_groups=mesh['dp'=4,'fsdp'=8] {'dp'}, use_global_device_ids=true, to_apply=%region_73.74 | all-reduce | flops 1152 | bytes 4608 | tf_op jit(solution)/shard_map/psum | solution.py:348
  599.5 60.8 %all-reduce.4.cloned.1.call-done = (bf16[8,64,512]{2,0,1:T(8,128)(2,1)}, bf16[8,64,512]{2,0,1:T(8,128)(2,1)}, bf16[64,2048]{1,0:T(8,128)(2,1)}, bf16[64,2048]{1,...) async-done(((bf16[8,64,512]{2,0,1:T(8,128)(2,1)}, bf16[8,64,512]{2,0,1:T(8,128)(2,1)}, bf16[64,2048]{1,0:T(8,128)(2,1)}, bf16[64,2048]{1,0:T(8,128)(2,1)}, ...) | async-done | bytes 2097168 | tf_op jit(solution)/shard_map/psum | solution.py:348
  (483 shorter events, 217.4 us)
Async XLA Ops:
  7.2 53.0 %all-gather.5.cloned.1.call-start = ((), (), s32[]{:S(2)}) async-start(), calls=%async_computation.8 | async-start | bytes 4718592 | tf_op jit(solution)/shard_map/all_gather | solution.py:304
  9.9 103.1 %all-gather.7.cloned.1.call-start = ((), (), s32[]{:S(2)}) async-start(), calls=%async_computation.9 | async-start | bytes 2359296 | tf_op jit(solution)/shard_map/all_gather | solution.py:305
  11.7 109.6 %all-gather.9.cloned.1.call-start = ((), (), s32[]{:S(2)}) async-start(), calls=%async_computation.10 | async-start | bytes 2359296 | tf_op jit(solution)/shard_map/all_gather | solution.py:306
  13.6 309.7 %reduce-scatter.21.cloned.1.call-start = ((), (), s32[]{:S(2)}) async-start(), calls=%async_computation.15 | async-start | bytes 4718592 | tf_op jit(solution)/shard_map/reduce_scatter | solution.py:344
  30.2 69.8 %copy-start.128 = (f32[1,512]{1,0:T(1,128)}, f32[1,512]{1,0:T(1,128)S(1)}, u32[]{:S(2)}) copy-start(f32[1,512]{1,0:T(1,128)S(1)} %get-tuple-element.189) | copy-start | bytes 6148
  30.2 91.1 %copy-start.130 = (f32[1,512]{1,0:T(1,128)}, f32[1,512]{1,0:T(1,128)S(1)}, u32[]{:S(2)}) copy-start(f32[1,512]{1,0:T(1,128)S(1)} %get-tuple-element.191) | copy-start | bytes 6148
  31.3 34.5 %copy-start.88 = (bf16[2,512,512]{2,1,0:T(8,128)(2,1)S(1)}, bf16[2,512,512]{2,1,0:T(8,128)(2,1)}, u32[]{:S(2)}) copy-start(bf16[2,512,512]{2,1,0:T(8,128)(2,1)} %param.16) | copy-start | bytes 3145732
  93.6 38.5 %copy-start.11 = (f32[512,512]{1,0:T(8,128)}, f32[512,512]{1,0:T(8,128)S(1)}, u32[]{:S(2)}) copy-start(f32[512,512]{1,0:T(8,128)S(1)} %get-tuple-element.227) | copy-start | bytes 3145732
  145.1 179.9 %reduce-scatter.23.cloned.1.call-start = ((), (), s32[]{:S(2)}) async-start(), calls=%async_computation.16 | async-start | bytes 4718592 | tf_op jit(solution)/shard_map/reduce_scatter | solution.py:344
  151.6 175.2 %reduce-scatter.19.cloned.1.call-start = ((), (), s32[]{:S(2)}) async-start(), calls=%async_computation.14 | async-start | bytes 4718592 | tf_op jit(solution)/shard_map/reduce_scatter | solution.py:343
  162.3 183.6 %reduce-scatter.17.cloned.1.call-start = ((), (), s32[]{:S(2)}) async-start(), calls=%async_computation.13 | async-start | bytes 4718592 | tf_op jit(solution)/shard_map/reduce_scatter | solution.py:343
  186.7 249.2 %reduce-scatter.15.cloned.1.call-start = ((), (), s32[]{:S(2)}) async-start(), calls=%async_computation.12 | async-start | bytes 9437184 | tf_op jit(solution)/shard_map/reduce_scatter | solution.py:342
  259.4 266.9 %reduce-scatter.13.cloned.1.call-start = ((), (), s32[]{:S(2)}) async-start(), calls=%async_computation.11 | async-start | bytes 9437184 | tf_op jit(solution)/shard_map/reduce_scatter | solution.py:342
  315.3 241.7 %reduce-scatter.25.cloned.1.call-start = ((), (), s32[]{:S(2)}) async-start(), calls=%async_computation.17 | async-start | bytes 294912
  319.3 268.6 %reduce-scatter.27.cloned.1.call-start = ((), (), s32[]{:S(2)}) async-start(), calls=%async_computation.18 | async-start | bytes 294912
  320.3 340.0 %all-reduce.4.cloned.1.call-start = ((), (), s32[]{:S(2)}) async-start(), calls=%async_computation.19 | async-start | bytes 4194304 | tf_op jit(solution)/shard_map/psum | solution.py:348
  328.6 202.2 %copy-start.49 = (bf16[8,64,512]{2,1,0:T(8,128)(2,1)S(1)}, bf16[8,64,512]{2,1,0:T(8,128)(2,1)}, u32[]{:S(2)}) copy-start(bf16[8,64,512]{2,1,0:T(8,128)(2,1)} %copy-done.48) | copy-start | bytes 1572868
  438.0 94.8 %copy-start.53 = (bf16[8,64,512]{2,1,0:T(8,128)(2,1)S(1)}, bf16[8,64,512]{2,1,0:T(8,128)(2,1)}, u32[]{:S(2)}) copy-start(bf16[8,64,512]{2,1,0:T(8,128)(2,1)} %copy-done.52) | copy-start | bytes 1572868
  537.8 61.0 %copy-start.125 = (f32[9,64]{1,0:T(8,128)S(1)}, f32[9,64]{1,0:T(8,128)}, u32[]{:S(2)}) copy-start(f32[9,64]{1,0:T(8,128)} %param.23) | copy-start | bytes 6916
  537.8 61.0 %copy-start.126 = (f32[9,64]{1,0:T(8,128)S(1)}, f32[9,64]{1,0:T(8,128)}, u32[]{:S(2)}) copy-start(f32[9,64]{1,0:T(8,128)} %param.30) | copy-start | bytes 6916
  537.8 61.0 %copy-start.127 = (f32[9,64]{1,0:T(8,128)S(1)}, f32[9,64]{1,0:T(8,128)}, u32[]{:S(2)}) copy-start(f32[9,64]{1,0:T(8,128)} %param.31) | copy-start | bytes 6916
  537.8 122.4 %copy-start.56 = (f32[8,64,512]{2,1,0:T(8,128)S(1)}, f32[8,64,512]{2,1,0:T(8,128)}, u32[]{:S(2)}) copy-start(f32[8,64,512]{2,1,0:T(8,128)} %param.20) | copy-start | bytes 3145732
  537.8 122.4 %copy-start.90 = (f32[8,64,512]{2,1,0:T(8,128)S(1)}, f32[8,64,512]{2,1,0:T(8,128)}, u32[]{:S(2)}) copy-start(f32[8,64,512]{2,1,0:T(8,128)} %param.24) | copy-start | bytes 3145732
  537.8 122.4 %copy-start.91 = (f32[8,64,512]{2,1,0:T(8,128)S(1)}, f32[8,64,512]{2,1,0:T(8,128)}, u32[]{:S(2)}) copy-start(f32[8,64,512]{2,1,0:T(8,128)} %param.25) | copy-start | bytes 3145732
  (133 other events, 621.7 us)
Sparse Core Ops, SparseCore 0:
  10.2 49.9 all-gather.4
  62.4 28.0 all-gather.6
  92.7 28.5 all-gather.8
  145.2 49.4 reduce-scatter.20
  196.9 48.1 reduce-scatter.22
  247.2 48.1 reduce-scatter.18
  297.7 48.1 reduce-scatter.16
  348.1 87.7 reduce-scatter.14
  438.2 87.9 reduce-scatter.12
  528.3 28.7 reduce-scatter.24
  559.4 28.3 reduce-scatter.26
  591.3 68.8 all-reduce.3
where the time goes:
time: 687 us; the launch traced here: 678 us
  waiting for transfers between devices  333 us (48%)
  matrix products  152 us (22%)
  local copies, waits for them, and re-layouts  91.4 us (13%)
  other arithmetic  57.5 us (8%)
  blocking collectives  25.9 us (4%)
  between operations  16.3 us (2%)
    reduce_scatter x2, waiting for transfers between devices, per_device(): lax.psum_scatter(micro_grads[0], 'fsdp', scatter_dimension=1, tiled=True)  177 us
    psum x1, waiting for transfers between devices, per_device(): lax.psum(shortened(shard_grads), 'dp')  60.8 us
    unnamed x14, waiting for transfers between devices  47.9 us
    unnamed x301, local copies, waits for them, and re-layouts  47.6 us
    dot_general x14, matrix products, across(): lax.dot_general(left_side, right_side, (((0,), (0,)), ((), ())), preferre...  35 us
    all_gather x1, waiting for transfers between devices, fetch_weights(): lax.all_gather(shards[0], 'fsdp', axis=1, tiled=True)  27.8 us
    dot_general x14, matrix products, against(): lax.dot_general(left_side, right_side, (((1,), (1,)), ((), ())), preferre...  26.2 us
    concatenate x2, local copies, waits for them, and re-layouts, layer_backward(): jnp.concatenate([projection_grads, out_one_grad[None], across(first_low,...  21 us
  transfers between devices with their start and end apart: 12, of which 8 were waited for; matrix products, arithmetic and copies ran while one was open for 35% of the time, Pallas kernels for 0%

commit v1 on v0

v1 whole, which is shorter than its diff:
```python
import math

import jax
import jax.numpy as jnp
from jax import lax
from jax.experimental import pallas as pl
from jax.experimental.pallas import tpu as pltpu
from jax.sharding import PartitionSpec as P

HEADS = 8
HEAD = 64
SLAB = 512
WIDTH = 512
PAIR = 2 * HEAD
STEP = 3
NORM_EPS = 1e-05
ADAM_EPS = 1e-08
LEARN_RATE = 0.2
FAR = -1e30
LOG2E = math.log2(math.e)
QSCALE = HEAD**-0.5 * LOG2E
TILE = 256
BF = jnp.bfloat16
F32 = jnp.float32
MIB = 1 << 20


def nn(a, b):
    return jnp.dot(a, b, preferred_element_type=F32)


def nt(a, b):
    return lax.dot_general(a, b, (((1,), (1,)), ((), ())), preferred_element_type=F32)


def tn(a, b):
    return lax.dot_general(a, b, (((0,), (0,)), ((), ())), preferred_element_type=F32)


def norm_forward(residual, eps=NORM_EPS):
    centred = residual - jnp.mean(residual, axis=-1, keepdims=True)
    spread = jnp.mean(centred * centred, axis=-1, keepdims=True)
    scale = lax.rsqrt(spread + eps)
    return centred * scale, scale


def norm_backward(upstream, unit, scale, gain):
    inner = upstream * gain
    first = jnp.mean(inner, axis=-1, keepdims=True)
    second = jnp.mean(inner * unit, axis=-1, keepdims=True)
    return scale * (inner - first - unit * second)


def rows_sum(values):
    return jnp.sum(values, axis=0, keepdims=True)


def attend_forward(k_ref, qt, vt, u, wt, e_ref, o_ref, r_ref, causal):
    lane = lax.broadcasted_iota(jnp.int32, (SLAB, PAIR), 1)
    low_half = lane < HEAD
    if causal:
        key_at = lax.broadcasted_iota(jnp.int32, (TILE, TILE), 0)
        query_at = lax.broadcasted_iota(jnp.int32, (TILE, TILE), 1)
        bias = jnp.where(key_at <= query_at, 0.0, FAR).astype(F32)
    for head in range(HEADS):
        pair = head // 2
        keys = k_ref[:, pair * PAIR : (pair + 1) * PAIR]
        query = qt[head * HEAD : (head + 1) * HEAD]
        value = vt[head * HEAD : (head + 1) * HEAD]
        if head % 2 == 0:
            left = jnp.where(low_half, keys, u)
            right = jnp.concatenate([query, wt], axis=0)
        else:
            left = jnp.where(low_half, u, keys)
            right = jnp.concatenate([wt, query], axis=0)
        for tile in range(SLAB // TILE):
            cols = slice(tile * TILE, (tile + 1) * TILE)
            depth = (tile + 1) * TILE if causal else SLAB
            scores = nn(left[:depth], right[:, cols])
            if causal:
                last = scores[tile * TILE :] + bias
                scores = last if tile == 0 else jnp.concatenate([scores[: tile * TILE], last], axis=0)
            top = jnp.max(scores, axis=0, keepdims=True)
            power = jnp.exp2(scores - top)
            inverse = 1.0 / jnp.sum(power, axis=0, keepdims=True)
            power = power.astype(BF)
            e_ref[head, :depth, cols] = power
            mix = nn(value[:, :depth], power) * inverse
            o_ref[head * HEAD : (head + 1) * HEAD, cols] = mix.astype(BF)
            r_ref[head : head + 1, cols] = inverse


def attend_backward(e_ref, r_ref, o_ref, qt_ref, kt_ref, v_ref, dmt, dqt_ref, dk_ref, dv_ref, causal):
    zero = jnp.zeros((HEAD, SLAB), BF)
    for pair in range(HEADS // 2):
        values = v_ref[:, pair * PAIR : (pair + 1) * PAIR]
        dk = [None] * (SLAB // TILE)
        dv = [None] * (SLAB // TILE)
        for side in range(2):
            head = 2 * pair + side
            rows = slice(head * HEAD, (head + 1) * HEAD)
            mixed = dmt[rows] * r_ref[head : head + 1, :]
            mixed = mixed.astype(BF)
            centre = jnp.sum(mixed.astype(F32) * o_ref[rows, :].astype(F32), axis=0, keepdims=True)
            query = qt_ref[rows, :]
            if side == 0:
                mixed = jnp.concatenate([mixed, zero], axis=0)
                query = jnp.concatenate([query, zero], axis=0)
            else:
                mixed = jnp.concatenate([zero, mixed], axis=0)
                query = jnp.concatenate([zero, query], axis=0)
            for tile in range(SLAB // TILE):
                cols = slice(tile * TILE, (tile + 1) * TILE)
                depth = (tile + 1) * TILE if causal else SLAB
                grad = nn(values[:depth], mixed[:, cols])
                power = e_ref[head, :depth, cols]
                score = (power.astype(F32) * (grad - centre[:, cols])).astype(BF)
                dqt_ref[rows, cols] = (nn(kt_ref[rows, :depth], score) * HEAD**-0.5).astype(BF)
                dv_now = nt(power, mixed[:, cols])
                dk_now = nt(score, query[:, cols])
                for part in range(depth // TILE):
                    span = slice(part * TILE, (part + 1) * TILE)
                    dv[part] = dv_now[span] if dv[part] is None else dv[part] + dv_now[span]
                    dk[part] = dk_now[span] if dk[part] is None else dk[part] + dk_now[span]
        for part in range(SLAB // TILE):
            span = slice(part * TILE, (part + 1) * TILE)
            dv_ref[span, pair * PAIR : (pair + 1) * PAIR] = dv[part].astype(BF)
            dk_ref[span, pair * PAIR : (pair + 1) * PAIR] = (dk[part] * (1.0 / LOG2E)).astype(BF)


def self_forward(x_ref, w_ref, vec_ref, u_ref, wt_ref, qt_ref, kt_ref, v_ref, e_ref, r_ref, o_ref, unit_ref, scale_ref, k_s):
    x = x_ref[0]
    qt = (nn(x, w_ref[0]) * QSCALE).astype(BF).T
    qt_ref[0] = qt
    keys = nn(x, w_ref[1]).astype(BF)
    k_s[...] = keys
    kt_ref[0] = keys.T
    values = nn(x, w_ref[2]).astype(BF)
    v_ref[0] = values
    attend_forward(k_s, qt, values.T, u_ref[0], wt_ref[0], e_ref.at[0], o_ref.at[0], r_ref.at[0], True)
    residual = vec_ref[6:7, :] * x.astype(F32) + tn(o_ref[0], w_ref[3])
    unit, scale = norm_forward(residual)
    unit_ref[0] = unit
    scale_ref[0] = scale


def cross_forward(unit1_ref, mem_ref, w_ref, vec_ref, u_ref, wt_ref, qt_ref, kt_ref, v_ref, e_ref, r_ref, o_ref, unit_ref, scale_ref, k_s):
    state = unit1_ref[0] * vec_ref[0:1, :] + vec_ref[3:4, :]
    memory = mem_ref[0]
    qt = (nn(state.astype(BF), w_ref[0]) * QSCALE).astype(BF).T
    qt_ref[0] = qt
    keys = nn(memory, w_ref[1]).astype(BF)
    k_s[...] = keys
    kt_ref[0] = keys.T
    values = nn(memory, w_ref[2]).astype(BF)
    v_ref[0] = values
    attend_forward(k_s, qt, values.T, u_ref[0], wt_ref[0], e_ref.at[0], o_ref.at[0], r_ref.at[0], False)
    residual = vec_ref[7:8, :] * state + tn(o_ref[0], w_ref[3])
    unit, scale = norm_forward(residual)
    unit_ref[0] = unit
    scale_ref[0] = scale


CUBE = 0.044715
ROOT = math.sqrt(2.0 / math.pi)


def feed_both(unit2_ref, cot_ref, ex_ref, co_ref, vec_ref, out_ref, ds_ref, dex_ref, dco_ref, dvec_ref, act_s, slope_s, dex_s, dco_s):
    step = pl.program_id(0)
    steps = pl.num_programs(0)
    hidden_width = ex_ref.shape[1]
    chunk = 512

    @pl.when(step == 0)
    def _():
        dex_s[...] = jnp.zeros_like(dex_s)
        dco_s[...] = jnp.zeros_like(dco_s)
        dvec_ref[...] = jnp.zeros_like(dvec_ref)

    state = unit2_ref[0] * vec_ref[1:2, :] + vec_ref[4:5, :]
    low = state.astype(BF)
    branch = None
    for part in range(hidden_width // chunk):
        cols = slice(part * chunk, (part + 1) * chunk)
        u = nn(low, ex_ref[:, cols])
        square = u * u
        bend = jnp.tanh(u * (ROOT + (ROOT * CUBE) * square))
        half = 0.5 + 0.5 * bend
        active = (u * half).astype(BF)
        act_s[:, cols] = active
        slope_s[:, cols] = half + (u * half) * (1.0 - bend) * (ROOT + (3.0 * ROOT * CUBE) * square)
        now = nn(active, co_ref[cols, :])
        branch = now if branch is None else branch + now
    unit, scale = norm_forward(vec_ref[8:9, :] * state + branch)
    out_ref[0] = (unit * vec_ref[2:3, :] + vec_ref[5:6, :]).astype(BF)
    up = cot_ref[0].astype(F32)
    dvec_ref[0:1, :] += rows_sum(up * unit)
    dvec_ref[1:2, :] += rows_sum(up)
    dres = norm_backward(up, unit, scale, vec_ref[2:3, :])
    dvec_ref[2:3, :] += rows_sum(dres * state)
    dstate = dres * vec_ref[8:9, :]
    dbranch = dres.astype(BF)
    low_t = low.T
    for part in range(hidden_width // chunk):
        cols = slice(part * chunk, (part + 1) * chunk)
        dco_s[cols, :] += tn(act_s[:, cols], dbranch)
        dhid = (nt(dbranch, co_ref[cols, :]) * slope_s[:, cols]).astype(BF)
        dex_s[:, cols] += nn(low_t, dhid)
        dstate = dstate + nt(dhid, ex_ref[:, cols])
    ds_ref[0] = dstate

    @pl.when(step == steps - 1)
    def _():
        dex_ref[...] = dex_s[...].astype(BF)
        dco_ref[...] = dco_s[...].astype(BF)


def cross_backward(ds2_ref, unit2_ref, scale2_ref, unit1_ref, mem_ref, w_ref, vec_ref, qt_ref, kt_ref, v_ref, e_ref, r_ref, o_ref,
                   dmem_ref, ds1_ref, dw_ref, dvec_ref, dqt_s, dk_s, dv_s, dw_s):
    step = pl.program_id(0)
    steps = pl.num_programs(0)

    @pl.when(step == 0)
    def _():
        dw_s[...] = jnp.zeros_like(dw_s)
        dvec_ref[...] = jnp.zeros_like(dvec_ref)

    up = ds2_ref[0]
    unit = unit2_ref[0]
    state = unit1_ref[0] * vec_ref[0:1, :] + vec_ref[3:4, :]
    dvec_ref[0:1, :] += rows_sum(up * unit)
    dvec_ref[1:2, :] += rows_sum(up)
    dres = norm_backward(up, unit, scale2_ref[0], vec_ref[1:2, :])
    dvec_ref[2:3, :] += rows_sum(dres * state)
    dbranch = dres.astype(BF)
    dw_s[3] += nn(o_ref[0], dbranch)
    dmt = nt(w_ref[3], dbranch)
    attend_backward(e_ref.at[0], r_ref.at[0], o_ref.at[0], qt_ref.at[0], kt_ref.at[0], v_ref.at[0], dmt, dqt_s, dk_s, dv_s, False)
    dq = dqt_s[...].T
    ds1_ref[0] = dres * vec_ref[7:8, :] + nt(dq, w_ref[0])
    dw_s[0] += nn(state.astype(BF).T, dq)
    memory_t = mem_ref[0].T
    dk = dk_s[...]
    dv = dv_s[...]
    dw_s[1] += nn(memory_t, dk)
    dw_s[2] += nn(memory_t, dv)
    dmem_ref[0] = nt(dk, w_ref[1]) + nt(dv, w_ref[2])

    @pl.when(step == steps - 1)
    def _():
        dw_ref[...] = dw_s[...].astype(BF)


def self_backward(ds1_ref, unit1_ref, scale1_ref, x_ref, w_ref, vec_ref, qt_ref, kt_ref, v_ref, e_ref, r_ref, o_ref,
                  dx_ref, dw_ref, dvec_ref, dqt_s, dk_s, dv_s, dw_s):
    step = pl.program_id(0)
    steps = pl.num_programs(0)

    @pl.when(step == 0)
    def _():
        dw_s[...] = jnp.zeros_like(dw_s)
        dvec_ref[...] = jnp.zeros_like(dvec_ref)

    up = ds1_ref[0]
    unit = unit1_ref[0]
    x = x_ref[0]
    dvec_ref[0:1, :] += rows_sum(up * unit)
    dvec_ref[1:2, :] += rows_sum(up)
    dres = norm_backward(up, unit, scale1_ref[0], vec_ref[0:1, :])
    dvec_ref[2:3, :] += rows_sum(dres * x.astype(F32))
    dbranch = dres.astype(BF)
    dw_s[3] += nn(o_ref[0], dbranch)
    dmt = nt(w_ref[3], dbranch)
    attend_backward(e_ref.at[0], r_ref.at[0], o_ref.at[0], qt_ref.at[0], kt_ref.at[0], v_ref.at[0], dmt, dqt_s, dk_s, dv_s, True)
    dq = dqt_s[...].T
    dk = dk_s[...]
    dv = dv_s[...]
    dx_ref[0] = dres * vec_ref[6:7, :] + nt(dq, w_ref[0]) + nt(dk, w_ref[1]) + nt(dv, w_ref[2])
    x_t = x.T
    dw_s[0] += nn(x_t, dq)
    dw_s[1] += nn(x_t, dk)
    dw_s[2] += nn(x_t, dv)

    @pl.when(step == steps - 1)
    def _():
        dw_ref[...] = dw_s[...].astype(BF)


def per_slab(*tail):
    return pl.BlockSpec((1,) + tail, lambda m: (m,) + (0,) * len(tail))


def fixed(*shape):
    return pl.BlockSpec(shape, lambda m: (0,) * len(shape))


def shape(dims, kind):
    return jax.ShapeDtypeStruct(tuple(dims), kind)


def params(mib):
    return pltpu.CompilerParams(dimension_semantics=("arbitrary",), vmem_limit_bytes=mib * MIB)


def attention_saved(g):
    return (
        [per_slab(WIDTH, SLAB), per_slab(WIDTH, SLAB), per_slab(SLAB, WIDTH), per_slab(HEADS, SLAB, SLAB), per_slab(HEADS, SLAB), per_slab(WIDTH, SLAB)],
        [shape((g, WIDTH, SLAB), BF), shape((g, WIDTH, SLAB), BF), shape((g, SLAB, WIDTH), BF), shape((g, HEADS, SLAB, SLAB), BF), shape((g, HEADS, SLAB), F32), shape((g, WIDTH, SLAB), BF)],
    )


def run_self_forward(x, w, vec, u, wt):
    g = x.shape[0]
    specs, shapes = attention_saved(g)
    return pl.pallas_call(
        self_forward,
        grid=(g,),
        in_specs=[per_slab(SLAB, WIDTH), fixed(4, WIDTH, WIDTH), fixed(16, WIDTH), per_slab(SLAB, PAIR), per_slab(HEAD, SLAB)],
        out_specs=specs + [per_slab(SLAB, WIDTH), per_slab(SLAB, 1)],
        out_shape=shapes + [shape((g, SLAB, WIDTH), F32), shape((g, SLAB, 1), F32)],
        scratch_shapes=[pltpu.VMEM((SLAB, WIDTH), BF)],
        compiler_params=params(48),
        name="self_forward",
    )(x, w, vec, u, wt)


def run_cross_forward(unit1, memory, w, vec, u, wt):
    g = memory.shape[0]
    specs, shapes = attention_saved(g)
    return pl.pallas_call(
        cross_forward,
        grid=(g,),
        in_specs=[per_slab(SLAB, WIDTH), per_slab(SLAB, WIDTH), fixed(4, WIDTH, WIDTH), fixed(16, WIDTH), per_slab(SLAB, PAIR), per_slab(HEAD, SLAB)],
        out_specs=specs + [per_slab(SLAB, WIDTH), per_slab(SLAB, 1)],
        out_shape=shapes + [shape((g, SLAB, WIDTH), F32), shape((g, SLAB, 1), F32)],
        scratch_shapes=[pltpu.VMEM((SLAB, WIDTH), BF)],
        compiler_params=params(48),
        name="cross_forward",
    )(unit1, memory, w, vec, u, wt)


def run_feed(unit2, cot, ex, co, vec):
    g = unit2.shape[0]
    ff = ex.shape[1]
    return pl.pallas_call(
        feed_both,
        grid=(g,),
        in_specs=[per_slab(SLAB, WIDTH), per_slab(SLAB, WIDTH), fixed(WIDTH, ff), fixed(ff, WIDTH), fixed(16, WIDTH)],
        out_specs=[per_slab(SLAB, WIDTH), per_slab(SLAB, WIDTH), fixed(WIDTH, ff), fixed(ff, WIDTH), fixed(8, WIDTH)],
        out_shape=[shape((g, SLAB, WIDTH), BF), shape((g, SLAB, WIDTH), F32), shape((WIDTH, ff), BF), shape((ff, WIDTH), BF), shape((8, WIDTH), F32)],
        scratch_shapes=[pltpu.VMEM((SLAB, ff), BF), pltpu.VMEM((SLAB, ff), F32), pltpu.VMEM((WIDTH, ff), F32), pltpu.VMEM((ff, WIDTH), F32)],
        compiler_params=params(56),
        name="feed_both",
    )(unit2, cot, ex, co, vec)


def backward_scratch():
    return [pltpu.VMEM((WIDTH, SLAB), BF), pltpu.VMEM((SLAB, WIDTH), BF), pltpu.VMEM((SLAB, WIDTH), BF), pltpu.VMEM((4, WIDTH, WIDTH), F32)]


def run_cross_backward(ds2, unit2, scale2, unit1, memory, w, vec, saved):
    g = memory.shape[0]
    specs, _ = attention_saved(g)
    return pl.pallas_call(
        cross_backward,
        grid=(g,),
        in_specs=[per_slab(SLAB, WIDTH), per_slab(SLAB, WIDTH), per_slab(SLAB, 1), per_slab(SLAB, WIDTH), per_slab(SLAB, WIDTH), fixed(4, WIDTH, WIDTH), fixed(16, WIDTH)] + specs,
        out_specs=[per_slab(SLAB, WIDTH), per_slab(SLAB, WIDTH), fixed(4, WIDTH, WIDTH), fixed(8, WIDTH)],
        out_shape=[shape((g, SLAB, WIDTH), F32), shape((g, SLAB, WIDTH), F32), shape((4, WIDTH, WIDTH), BF), shape((8, WIDTH), F32)],
        scratch_shapes=backward_scratch(),
        compiler_params=params(56),
        name="cross_backward",
    )(ds2, unit2, scale2, unit1, memory, w, vec, *saved)


def run_self_backward(ds1, unit1, scale1, x, w, vec, saved):
    g = x.shape[0]
    specs, _ = attention_saved(g)
    return pl.pallas_call(
        self_backward,
        grid=(g,),
        in_specs=[per_slab(SLAB, WIDTH), per_slab(SLAB, WIDTH), per_slab(SLAB, 1), per_slab(SLAB, WIDTH), fixed(4, WIDTH, WIDTH), fixed(16, WIDTH)] + specs,
        out_specs=[per_slab(SLAB, WIDTH), fixed(4, WIDTH, WIDTH), fixed(8, WIDTH)],
        out_shape=[shape((g, SLAB, WIDTH), F32), shape((4, WIDTH, WIDTH), BF), shape((8, WIDTH), F32)],
        scratch_shapes=backward_scratch(),
        compiler_params=params(56),
        name="self_backward",
    )(ds1, unit1, scale1, x, w, vec, *saved)


def piece_bounds(lengths):
    closing = jnp.cumsum(lengths, axis=-1)
    opening = closing - lengths
    pad = ((0, 0), (0, 0), (0, HEAD - lengths.shape[-1]))
    return jnp.pad(opening, pad), jnp.pad(closing, pad)


def mask_factors(lengths):
    opening, closing = piece_bounds(lengths)
    places = jnp.arange(SLAB, dtype=jnp.int32)
    keys = (opening[:, :, None, :] <= places[:, None]) & (places[:, None] < closing[:, :, None, :])
    keys = jnp.concatenate([keys, keys], axis=-1).astype(BF)
    inside = (opening[:, 0, :, None] <= places) & (places < closing[:, 0, :, None])
    queries = jnp.where(inside, 0.0, FAR).astype(BF)
    return keys[:, 0], keys[:, 1], queries


def adam_update(weight, first_moment, second_moment, gradient, correction):
    first_next = 0.5 * first_moment + 0.5 * gradient
    second_next = 0.5 * second_moment + 0.5 * gradient * gradient
    weight_next = weight - LEARN_RATE * (first_next / correction) / (jnp.sqrt(second_next / correction) + ADAM_EPS)
    return (weight_next, first_next, second_next)


def padded_rows(flat):
    short = -flat.shape[-1] % (16 * WIDTH)
    flat = jnp.pad(flat, ((0, 0), (0, short)))
    return flat.reshape(flat.shape[0], -1, WIDTH)


def stacked_blocks(full, n):
    return full.reshape(full.shape[0], n, -1, WIDTH).transpose(1, 0, 2, 3).reshape(n, -1, WIDTH)


def unstacked(blocks, count):
    n = blocks.shape[0]
    return blocks.reshape(n, count, -1, WIDTH).transpose(1, 0, 2, 3).reshape(count, -1, WIDTH)


def gather(shard):
    return lax.all_gather(shard, "fsdp", axis=0)


def reduce(blocks):
    mine = lax.psum_scatter(blocks, "fsdp", scatter_dimension=0, tiled=False)
    return lax.psum(mine, "dp")


def per_device(
    inputs,
    memory,
    cotangent,
    lengths,
    stacked_weights,
    expand_weights,
    contract_weights,
    scale_vectors,
    stacked_first,
    stacked_second,
    expand_first,
    expand_second,
    contract_first,
    contract_second,
    vector_first,
    vector_second,
):
    n = lax.axis_size("fsdp")
    width = WIDTH // n
    micro = inputs.shape[0]
    slabs = micro * lengths.shape[1]
    x = inputs.reshape(slabs, SLAB, WIDTH)
    mem = memory.reshape(slabs, SLAB, WIDTH)
    cot = cotangent.reshape(slabs, SLAB, WIDTH)
    u_self, u_cross, wt = mask_factors(lengths.reshape(slabs, 2, -1))

    vector_shard = padded_rows(scale_vectors.astype(BF).reshape(1, -1))[0]
    stacked_low = stacked_weights.astype(BF)
    head_shard = jnp.concatenate([stacked_low[:4].reshape(-1, WIDTH), vector_shard], axis=0)
    got_self = gather(head_shard)
    got_cross = gather(stacked_low[4:].reshape(-1, WIDTH))
    got_feed = gather(jnp.concatenate([expand_weights.astype(BF).reshape(-1, WIDTH), contract_weights.astype(BF)], axis=0))
    w_self = unstacked(got_self[:, : 4 * width], 4)
    vec = got_self[:, 4 * width :].reshape(n, -1)[:, : 9 * width].reshape(n, 9, width).transpose(1, 0, 2).reshape(9, WIDTH)
    vec = jnp.pad(vec.astype(F32), ((0, 7), (0, 0)))
    w_cross = unstacked(got_cross, 4)
    hidden = expand_weights.shape[1]
    rows = width * hidden // WIDTH
    ex = got_feed[:, :rows].reshape(WIDTH, hidden)
    co = got_feed[:, rows:].reshape(hidden, WIDTH)

    *saved1, unit1, scale1 = run_self_forward(x, w_self, vec, u_self, wt)
    *saved2, unit2, scale2 = run_cross_forward(unit1, mem, w_cross, vec, u_cross, wt)
    out, ds2, dex, dco, dvec3 = run_feed(unit2, cot, ex, co, vec)
    grad_feed = reduce(jnp.concatenate([dex.reshape(n, rows, WIDTH), dco.reshape(n, -1, WIDTH)], axis=1))
    dmem, ds1, dw_cross, dvec2 = run_cross_backward(ds2, unit2, scale2, unit1, mem, w_cross, vec, saved2)
    grad_cross = reduce(stacked_blocks(dw_cross, n))
    dx, dw_self, dvec1 = run_self_backward(ds1, unit1, scale1, x, w_self, vec, saved1)
    dvec = jnp.stack([d[row] for row in range(3) for d in (dvec1, dvec2, dvec3)])
    dvec = padded_rows(dvec.astype(BF).reshape(9, n, width).transpose(1, 0, 2).reshape(n, -1))
    grad_self = reduce(jnp.concatenate([stacked_blocks(dw_self, n), dvec], axis=1))

    grad_stacked = jnp.concatenate([grad_self[: 4 * width].reshape(4, width, WIDTH), grad_cross.reshape(4, width, WIDTH)], axis=0)
    grad_vector = grad_self[4 * width :].reshape(-1)[: 9 * width].reshape(9, width)
    grad_expand = grad_feed[:rows].reshape(width, hidden)
    grad_contract = grad_feed[rows:]
    correction = 1.0 - 0.5**STEP
    params_now = (stacked_weights, expand_weights, contract_weights, scale_vectors)
    firsts = (stacked_first, expand_first, contract_first, vector_first)
    seconds = (stacked_second, expand_second, contract_second, vector_second)
    grads = (grad_stacked, grad_expand, grad_contract, grad_vector)
    updates = [adam_update(p, f, s, g.astype(F32), correction) for p, f, s, g in zip(params_now, firsts, seconds, grads)]
    return (
        out.reshape(inputs.shape),
        dx.reshape(inputs.shape),
        dmem.reshape(inputs.shape),
        updates[0][0],
        updates[1][0],
        updates[2][0],
        updates[3][0],
        updates[0][1],
        updates[0][2],
        updates[1][1],
        updates[1][2],
        updates[2][1],
        updates[2][2],
        updates[3][1],
        updates[3][2],
    )


def solution(mesh):
    tokens = P(None, ("dp", "fsdp"), None)
    pieces = P(None, ("dp", "fsdp"), None, None)
    stacked = P(None, "fsdp", None)
    rows = P("fsdp", None)
    columns = P(None, "fsdp")
    return jax.shard_map(
        per_device,
        mesh=mesh,
        in_specs=(tokens, tokens, tokens, pieces, stacked, rows, rows, columns) + (stacked, stacked, rows, rows, rows, rows, columns, columns),
        out_specs=(tokens, tokens, tokens, stacked, rows, rows, columns) + (stacked, stacked, rows, rows, rows, rows, columns, columns),
        check_vma=False,
    )
```

time: 687 us -> 388 us (0.56)
  matrix products: 152 us -> 0 us
  waiting for transfers between devices: 333 us -> 200 us
  Pallas kernels: 0 us -> 111 us
  local copies, waits for them, and re-layouts: 91.4 us -> 37.9 us
  other arithmetic: 57.5 us -> 17.4 us
  blocking collectives: 25.9 us -> 0 us
    dot_general x70 -> x0, matrix products: 152 us -> none  [the longest x14 35 us: across(): lax.dot_general(left_side, right_side, (((0,), (0,)), ((), ())), preferre...]
    pallas_call x0 -> x5, Pallas kernels: none -> 111 us  [the longest x1 27.7 us: run_cross_backward(): pl.pallas_call(cross_backward, grid=(g,), in_specs=[per_slab(SLAB, WIDTH)...]
    reduce_scatter x6 -> x3, waiting for transfers between devices: 194 us -> 86.8 us  [reduce(): mine = lax.psum_scatter(blocks, 'fsdp', scatter_dimension=0, tiled=False)]
    unnamed x14 -> x7, waiting for transfers between devices: 47.9 us -> 0.11 us
    unnamed x301 -> x67, local copies, waits for them, and re-layouts: 47.6 us -> 12.4 us
    all_gather x3, waiting for transfers between devices: 31 us -> 58 us  [gather(): return lax.all_gather(shard, 'fsdp', axis=0)]
    convert_element_type x13 -> x7, other arithmetic: 29.7 us -> 2.87 us  [the longest x1 1.34 us: per_device(): stacked_low = stacked_weights.astype(BF)]
    concatenate x2 -> x0, local copies, waits for them, and re-layouts: 21 us -> none  [layer_backward(): jnp.concatenate([projection_grads, out_one_grad[None], across(first_low,...]
  transfers between devices with their start and end apart: 12 -> 7, of which waited for: 8 -> 5; matrix products, arithmetic and copies ran while one was open for 35% -> 6% of each run, Pallas kernels for 0% -> 16%
where the time goes in v1:
time: 388 us; the launch traced here: 382 us
  waiting for transfers between devices  200 us (52%)
  Pallas kernels  111 us (29%)
  local copies, waits for them, and re-layouts  37.9 us (10%)
  other arithmetic  17.4 us (4%)
  between operations  14.8 us (4%)
    reduce_scatter x3, waiting for transfers between devices, reduce(): mine = lax.psum_scatter(blocks, 'fsdp', scatter_dimension=0, tiled=False)  86.8 us
    all_gather x3, waiting for transfers between devices, gather(): return lax.all_gather(shard, 'fsdp', axis=0)  58 us
    psum x1, waiting for transfers between devices, reduce(): return lax.psum(mine, 'dp')  55.3 us
    pallas_call x1, Pallas kernels, run_cross_backward(): pl.pallas_call(cross_backward, grid=(g,), in_specs=[per_slab(SLAB, WIDTH)...  27.7 us
    pallas_call x1, Pallas kernels, run_self_backward(): pl.pallas_call(self_backward, grid=(g,), in_specs=[per_slab(SLAB, WIDTH),...  24.7 us
    pallas_call x1, Pallas kernels, run_feed(): pl.pallas_call(feed_both, grid=(g,), in_specs=[per_slab(SLAB, WIDTH), per...  23.5 us
    pallas_call x1, Pallas kernels, run_cross_forward(): pl.pallas_call(cross_forward, grid=(g,), in_specs=[per_slab(SLAB, WIDTH),...  20.2 us
    pallas_call x1, Pallas kernels, run_self_forward(): pl.pallas_call(self_forward, grid=(g,), in_specs=[per_slab(SLAB, WIDTH),...  15.2 us
  transfers between devices with their start and end apart: 7, of which 5 were waited for; matrix products, arithmetic and copies ran while one was open for 6% of the time, Pallas kernels for 16%

profile of v1, /device:TPU:0, one launch (start us, length us, event | category | flops | bytes accessed | tf_op | source)
XLA Modules:
  0.0 381.9 jit_solution(18030771136834464424)
XLA Ops:
  7.2 1.3 convert_element_type.51
  12.8 29.2 %all-gather.6.cloned.1.call-done = bf16[8,256,512]{2,1,0:T(8,128)(2,1)} async-done(((bf16[1,256,512]{2,1,0:T(8,128)(2,1)}), bf16[8,256,512]{2,1,0:T(8,128)(2,1)}) %all-gather.6.cloned.1.call-update) | async-done | bytes 2097168 | tf_op jit(solution)/shard_map/all_gather | solution.py:431
  42.0 3.1 copy.53
  45.2 28.8 %all-gather.8.cloned.1.call-done = bf16[2176,512]{1,0:T(8,128)(2,1)} async-done(((bf16[272,512]{1,0:T(8,128)(2,1)}), bf16[2176,512]{1,0:T(8,128)(2,1)}) %all-gather.8.cloned.1.call-update) | async-done | bytes 2228240 | tf_op jit(solution)/shard_map/all_gather | solution.py:431
  74.0 1.8 slice.114
  75.8 1.6 copy.49
  78.7 15.2 %self_forward.1 = (bf16[2,512,512]{2,1,0:T(8,128)(2,1)S(1)}, bf16[2,512,512]{2,1,0:T(8,128)(2,1)S(1)}, bf16[2,512,512]{2,1,0:T(8,128)(2,1)S(1)}, bf16[2,8,512,51...) custom-call(bf16[2,512,512]{2,1,0:T(8,128)(2,1)S(1)} %copy-done, ...), custom_call_target="tpu_custom_call" | custom-call | tf_op jit(solution)/shard_map/self_forward/pallas_call | solution.py:315
  99.3 20.2 %cross_forward.1 = (bf16[2,512,512]{2,1,0:T(8,128)(2,1)S(1)}, bf16[2,512,512]{2,1,0:T(8,128)(2,1)S(1)}, bf16[2,512,512]{2,1,0:T(8,128)(2,1)S(1)}, bf16[2,8,512,5...) custom-call(f32[2,512,512]{2,1,0:T(8,128)} %get-tuple-element.43.uni, ...), custom_call_target="tpu_custom_call" | custom-call | tf_op jit(solution)/shard_map/cross_forward/pallas_call | solution.py:330
  124.7 3.9 %fusion.10 = (bf16[8,256,512]{2,1,0:T(8,128)(2,1)}, bf16[8,256,512]{2,1,0:T(8,128)(2,1)S(1)}) fusion(bf16[8,512,512]{2,1,0:T(8,128)(2,1)} %bitcast.51), kind=kLoop, calls=%fused_computation.48 | loop fusion | bytes 8388608 | tf_op jit(solution)/shard_map/slice | solution.py:479
  128.7 2.6 reshape.138.ex_ref
  131.3 23.5 %feed_both.1 = (bf16[2,512,512]{2,1,0:T(8,128)(2,1)}, f32[2,512,512]{2,1,0:T(8,128)}, bf16[512,2048]{1,0:T(8,128)(2,1)}, bf16[2048,512]{1,0:T(8,128)(2,1)}, f32[8,512]{1,0:T(8,128)}) custom-call(f32[2,512,512]{2,1,0:T(8,128)} %get-tuple-element.44.unit2_ref, bf16[2,512,512]{2,1,0:T(8,128)(2,1)} %cot_ref.1, bf16[512,2048]{1,0:T(8,128)(2,1)} %reshape.138.ex_ref, ...), custom_call_target="tpu_custom_call" | custom-call | tf_op jit(solution)/shard_map/feed_both/pallas_call | solution.py:345
  154.8 27.7 %cross_backward.1 = (f32[2,512,512]{2,1,0:T(8,128)}, f32[2,512,512]{2,1,0:T(8,128)}, bf16[4,512,512]{2,1,0:T(8,128)(2,1)}, f32[8,512]{1,0:T(8,128)}) custom-call(f32[2,512,512]{2,1,0:T(8,128)} %get-tuple-element.46.ds2_ref, f32[2,512,512]{2,1,0:T(8,128)} %get-tuple-element.44.unit2_ref, f32[2,512,1]{2,1,0:T(8,128)} %copy-done.12, ...), custom_call_target="tpu_custom_call" | custom-call | tf_op jit(solution)/shard_map/cross_backward/pallas_call | solution.py:364
  182.6 3.2 copy.64
  185.8 24.7 %self_backward.1 = (f32[2,512,512]{2,1,0:T(8,128)}, bf16[4,512,512]{2,1,0:T(8,128)(2,1)}, f32[8,512]{1,0:T(8,128)}) custom-call(f32[2,512,512]{2,1,0:T(8,128)} %get-tuple-element.54.ds1_ref, f32[2,512,512]{2,1,0:T(8,128)} %get-tuple-element.43.unit1_ref, f32[2,512,1]{2,1,0:T(8,128)} %copy-done.11, bf16[2,512,512]{2,1,0:T(8,128)(2,1)} %x_ref.3, ...), custom_call_target="tpu_custom_call" | custom-call | tf_op jit(solution)/shard_map/self_backward/pallas_call | solution.py:379
  210.6 1.8 copy.54
  213.5 1.6 pad_maximum_fusion.1
  215.2 3.1 reshape.148
  218.3 4.0 %pad_maximum_fusion = bf16[8,512,512]{2,1,0:T(8,128)(2,1)} fusion(bf16[8,256,512]{2,1,0:T(8,128)(2,1)} %bitcast.57, bf16[8,256,512]{2,1,0:T(8,128)(2,1)S(1)} %reshape.148), kind=kLoop, calls=%fused_computation | loop fusion | flops 8388608 | bytes 8388608 | tf_op jit(solution)/shard_map/concatenate | solution.py:484
  222.4 35.5 %reduce-scatter.4.cloned.1.call-done = bf16[1,272,512]{2,1,0:T(8,128)(2,1)} async-done(((bf16[8,272,512]{2,1,0:T(8,128)(2,1)}), bf16[1,272,512]{2,1,0:T(8,128)(2,1)}) %reduce-scatter.4.cloned.1.call-update) | async-done | bytes 278544 | tf_op jit(solution)/shard_map/reduce_scatter | solution.py:435
  257.9 51.3 %reduce-scatter.8.cloned.1.call-done = bf16[1,512,512]{2,1,0:T(8,128)(2,1)} async-done(((bf16[8,512,512]{2,1,0:T(8,128)(2,1)}), bf16[1,512,512]{2,1,0:T(8,128)(2,1)}) %reduce-scatter.8.cloned.1.call-update) | async-done | bytes 524304 | tf_op jit(solution)/shard_map/reduce_scatter | solution.py:435
  309.2 55.3 %all-reduce.8.cloned.1.call-done = (bf16[4,64,512]{2,1,0:T(8,128)(2,1)}, bf16[272,512]{1,0:T(8,128)(2,1)}, bf16[512,512]{1,0:T(8,128)(2,1)}) async-done(((bf16[4,64,512]{2,1,0:T(8,128)(2,1)}, bf16[272,512]{1,0:T(8,128)(2,1)}, bf16[512,512]{1,0:T(8,128)(2,1)}), (bf16[4,64,512]{2,1,0:T(8,128)(2,1)}, bf16[272,512]{1,0:T(8,128)(2,1)}, bf16[512,512]{1,0:T(8,128)(2,1)})) %all-reduce.8.cloned.1.call-update) | async-done | bytes 1064976 | tf_op jit(solution)/shard_map/psum | solution.py:436
  367.6 2.7 divide_subtract_fusion.1
  370.9 1.4 divide_subtract_fusion.2
  372.7 2.1 divide_subtract_fusion
  (131 shorter events, 21.6 us)
Async XLA Ops:
  7.2 2.3 copy-start.24
  7.2 3.2 copy-start.16
  7.2 34.8 %all-gather.6.cloned.1.call-start = ((), (), s32[]{:S(2)}) async-start(), calls=%async_computation.3 | async-start | bytes 2359296 | tf_op jit(solution)/shard_map/all_gather | solution.py:431
  8.6 2.0 copy-start.17
  9.4 64.6 %all-gather.8.cloned.1.call-start = ((), (), s32[]{:S(2)}) async-start(), calls=%async_computation.7 | async-start | bytes 2506752 | tf_op jit(solution)/shard_map/all_gather | solution.py:431
  10.4 114.4 %all-gather.10.cloned.1.call-start = ((), (), s32[]{:S(2)}) async-start(), calls=%async_computation.8 | async-start | bytes 4718592 | tf_op jit(solution)/shard_map/all_gather | solution.py:431
  11.5 210.9 %reduce-scatter.6.cloned.1.call-start = ((), (), s32[]{:S(2)}) async-start(), calls=%async_computation.5 | async-start | bytes 2359296 | tf_op jit(solution)/shard_map/reduce_scatter | solution.py:435
  75.8 2.9 copy-start
  77.4 21.9 %copy-start.1 = (bf16[2,512,512]{2,1,0:T(8,128)(2,1)S(1)}, bf16[2,512,512]{2,1,0:T(8,128)(2,1)}, u32[]{:S(2)}) copy-start(bf16[2,512,512]{2,1,0:T(8,128)(2,1)} %mem_ref.3) | copy-start | bytes 3145732
  78.7 40.7 %copy-start.2 = (f32[16,512]{1,0:T(8,128)}, f32[16,512]{1,0:T(8,128)S(1)}, u32[]{:S(2)}) copy-start(f32[16,512]{1,0:T(8,128)S(1)} %pad_convert_fusion.vec_ref) | copy-start | bytes 98308
  185.8 72.1 %reduce-scatter.4.cloned.1.call-start = ((), (), s32[]{:S(2)}) async-start(), calls=%async_computation.4 | async-start | bytes 2506752 | tf_op jit(solution)/shard_map/reduce_scatter | solution.py:435
  210.5 2.1 copy-start.26
  210.5 2.4 copy-start.25
  215.2 94.1 %reduce-scatter.8.cloned.1.call-start = ((), (), s32[]{:S(2)}) async-start(), calls=%async_computation.6 | async-start | bytes 4718592 | tf_op jit(solution)/shard_map/reduce_scatter | solution.py:435
  222.3 145.3 %copy-start.18 = (f32[256,512]{1,0:T(8,128)S(1)}, f32[256,512]{1,0:T(8,128)}, u32[]{:S(2)}) copy-start(f32[256,512]{1,0:T(8,128)} %param.22) | copy-start | bytes 1572868
  222.3 142.2 %all-reduce.8.cloned.1.call-start = ((), (), s32[]{:S(2)}) async-start(), calls=%async_computation.9 | async-start | bytes 2129920 | tf_op jit(solution)/shard_map/psum | solution.py:436
  367.3 3.0 copy-start.29
  367.3 3.0 copy-start.30
  367.3 3.6 copy-start.21
  367.3 3.6 copy-start.22
  370.2 2.0 copy-start.15
  370.2 2.0 copy-start.19
  370.3 2.2 copy-start.20
  370.3 2.4 copy-start.23
  (14 other events, 13.8 us)
Sparse Core Ops, SparseCore 0:
  10.2 31.7 all-gather.5
  44.3 29.6 all-gather.7
  76.1 46.5 all-gather.9
  185.9 35.2 reduce-scatter.5
  223.4 34.5 reduce-scatter.3
  260.2 48.9 reduce-scatter.7
  312.9 51.5 all-reduce.7
